TPU v7x, 32 devices: a whole 2x2x4 slice. The times are simulated.
32 devices in a mesh: dp: 4 (over y, x), seq: 8 (over z, core).
Axes of the slice: x: 2, y: 2, z: 4, core: 2. Of those that a mesh axis runs over, the one named last changes fastest.
Arguments:
- inputs: bfloat16 [4096, 6144], P('seq'), may hold values from -6 to 6
- qkv_weight: bfloat16 [6144, 12288], P(None, ('dp', 'seq')), may hold values from -0.078125 to 0.078125
- log_decay: float32 [32, 4096], P('dp', 'seq'), may hold values from -1 to 0, as said below
- out_gain: float32 [32, 128], P('dp'), may hold values from 0.1 to 1.9
Outputs:
- attended: bfloat16 [4096, 4096], P('seq', 'dp')
Inputs may be any that keep to these rules, and one draw needn't show every extreme that they name: `log_decay`: log of a decay factor, negative at every position.
All inputs are finite; a program needn't handle non-finite values.
Results may differ from a plain program's by a relative error of at most 0.0055.
Values may be sent and summed in bfloat16 or wider, within the bound.
A program may use at most 128 MiB of HBM per device.

v0:
```python
import jax
import jax.numpy as jnp
from jax import lax
from jax.sharding import PartitionSpec as P


def prefix_2(value, axis, join, neutral):
    count, mine = (lax.axis_size(axis), lax.axis_index(axis))
    pieces = jax.tree.map(lambda part: lax.all_gather(part, axis), value)
    subtotal = jax.tree.map(
        lambda part, zero: jnp.full_like(part, 0) + jnp.asarray(zero, part.dtype), value, neutral
    )

    def turn(position, subtotal):
        longer = join(subtotal, jax.tree.map(lambda part: part[position], pieces))
        return jax.tree.map(lambda new, old: jnp.where(position < mine, new, old), longer, subtotal)

    return lax.fori_loop(0, count - 1, turn, subtotal)


def block_terms(queries, keys, values, block_decay):
    cumulated = jnp.cumsum(block_decay, axis=-1)
    tok_count = queries.shape[-2]
    row_index = jnp.arange(tok_count)[:, None]
    col_index = jnp.arange(tok_count)[None, :]
    causal = row_index >= col_index
    spread = cumulated[:, :, None] - cumulated[:, None, :]
    decay_mask = jnp.where(causal, jnp.exp(jnp.where(causal, spread, 0.0)), 0.0)
    scores = jnp.einsum("htd,hsd->hts", queries, keys, preferred_element_type=jnp.float32)
    weights = (scores * decay_mask).astype(jnp.bfloat16)
    intra_term = jnp.einsum("hts,hsd->htd", weights, values, preferred_element_type=jnp.float32)
    tail_decay = jnp.exp(cumulated[:, -1:] - cumulated)
    keys_decayed = keys.astype(jnp.float32) * tail_decay[:, :, None]
    update = jnp.einsum(
        "hsd,hse->hde", keys_decayed, values.astype(jnp.float32), precision=lax.Precision.HIGHEST
    )
    block_total = cumulated[:, -1]
    queries_decayed = queries.astype(jnp.float32) * jnp.exp(cumulated)[:, :, None]
    return (intra_term, update, block_total, queries_decayed)


def finish_heads(intra_term, queries_decayed, carried, gains):
    outer_term = jnp.einsum(
        "htd,hde->hte", queries_decayed, carried, precision=lax.Precision.HIGHEST
    )
    combined = intra_term + outer_term
    root_mean = lax.rsqrt(jnp.mean(combined * combined, axis=-1, keepdims=True) + 1e-05)
    return combined * root_mean * gains[:, None, :]


def chain_combine(earlier_pair, later_pair):
    return (
        earlier_pair[0] + later_pair[0],
        jnp.exp(later_pair[0])[:, None, None] * earlier_pair[1] + later_pair[1],
    )


def shards(inputs, qkv_weight, log_decay, out_gain):
    tok_count = inputs.shape[0]
    local_heads = out_gain.shape[0]
    head_size = out_gain.shape[1]
    projected = jnp.dot(
        inputs,
        lax.all_gather(qkv_weight, "seq", axis=1, tiled=True),
        preferred_element_type=jnp.float32,
    )
    activated = jax.nn.silu(projected).astype(jnp.bfloat16)
    grouped = jnp.transpose(activated.reshape(tok_count, local_heads, 3, head_size), (2, 1, 0, 3))
    intra_term, update, block_total, queries_decayed = block_terms(
        grouped[0], grouped[1], grouped[2], log_decay
    )
    identity = (jnp.zeros_like(block_total), jnp.zeros_like(update))
    prefix = prefix_2((block_total, update), "seq", chain_combine, identity)
    normed = finish_heads(intra_term, queries_decayed, prefix[1], out_gain)
    return (
        jnp.transpose(normed, (1, 0, 2))
        .reshape(tok_count, local_heads * head_size)
        .astype(jnp.bfloat16)
    )


def solution(mesh):
    in_specs = (P("seq", None), P(None, ("dp", "seq")), P("dp", "seq"), P("dp", None))
    out_specs = P("seq", "dp")
    return jax.shard_map(shards, mesh=mesh, in_specs=in_specs, out_specs=out_specs, check_vma=False)
```

profile of v0, /device:TPU:11, one launch (start us, length us, event | category | flops | bytes accessed | tf_op | source)
XLA Modules:
  0.0 439.8 jit_solution(11498574792190380569)
XLA Ops:
  6.5 0.7 all-gather.5.cloned.1.call-update
  7.3 0.0 all-gather.7.cloned.1.call-start
  7.3 1.1 reduce-window.6
  8.5 0.2 slice_reduce_fusion
  8.7 0.1 fusion.19
  8.7 0.2 slice_reduce_fusion.1
  8.9 0.1 subtract_exponential_fusion
  9.0 323.7 %all-gather.5.cloned.1.call-done = bf16[6144,3072]{1,0:T(8,128)(2,1)} async-done(((bf16[6144,384]{1,0:T(8,128)(2,1)}), bf16[6144,3072]{1,0:T(8,128)(2,1)}) %all-gather.5.cloned.1.call-update) | async-done | bytes 37748752 | tf_op jit(solution)/shard_map/all_gather | solution.py:64
  332.7 28.1 %multiply_convert_fusion.1 = bf16[512,3072]{1,0:T(8,128)(2,1)} fusion(bf16[512,6144]{1,0:T(8,128)(2,1)} %param.6, bf16[6144,3072]{1,0:T(8,128)(2,1)} %all-gather.5.cloned.1.call-done), kind=kOutput, calls=%fused_computation.4 | convolution fusion | flops 19335217152 | bytes 47185920 | tf_op jit(solution)/shard_map/dot_general | solution.py:62
  360.9 3.2 copy.26
  364.0 2.8 copy.27
  366.9 4.8 %fusion.7 = f32[8,128,128]{2,1,0:T(8,128)} fusion(f32[8,512]{1,0:T(8,128)S(1)} %subtract_exponential_fusion, bf16[3,8,512,128]{3,2,1,0:T(8,128)(2,1)} %bitcast.51), kind=kOutput, calls=%fused_computation.12 | convolution fusion | flops 806354944 | bytes 2637824 | tf_op jit(solution)/shard_map/hsd,hse->hde/dot_general | solution.py:34
  371.7 0.0 all-gather.7.cloned.1.call-update
  371.7 0.6 dynamic-slice
  373.0 0.2 dynamic-update-slice
  373.2 12.0 %all-reduce = f32[64]{0:T(128)S(1)} all-reduce(f32[64]{0:T(128)S(1)} %dynamic-update-slice), channel_id=2, replica_groups=mesh['dp'=4,'seq'=8] {'seq'}, use_global_device_ids=true, to_apply=%add | all-reduce | flops 64 | bytes 512
  385.2 0.1 reshape.90
  385.2 0.1 iota_compare_fusion
  385.3 5.8 %fusion.1 = f32[8,512,128]{1,2,0:T(8,128)S(1)} fusion(f32[8,512]{1,0:T(8,128)S(1)} %get-tuple-element.129, pred[512,512]{1,0:T(8,128)(4,1)S(1)} %iota_compare_fusion, bf16[3,8,512,128]{3,2,1,0:T(8,128)(2,1)} %bitcast.52), kind=kOutput, calls=%fused_computation.5 | convolution fusion | flops 1084227584 | bytes 5537792 | tf_op jit(solution)/shard_map/hts,hsd->htd/dot_general | solution.py:31
  391.1 27.7 %all-gather.7.cloned.1.call-done = f32[64,128,128]{2,1,0:T(8,128)} async-done(((f32[8,128,128]{2,1,0:T(8,128)}), f32[64,128,128]{2,1,0:T(8,128)}) %all-gather.7.cloned.1.call-update) | async-done | bytes 4194320 | tf_op jit(solution)/shard_map/all_gather | solution.py:9
  418.8 8.5 %while.14 = (s32[]{:T(128)}, f32[8,128,128]{2,1,0:T(8,128)S(1)}, s32[]{:T(128)}, f32[8,8]{1,0:T(8,128)S(1)}, f32[8,8,128,128]{3,2,1,0:T(8,128)}, /*index=5*/s32[]{:T(128)}, s32[]{:T(128)}) while((s32[]{:T(128)}, f32[8,128,128]{2,1,0:T(8,128)S(1)}, s32[]{:T(128)}, f32[8,8]{1,0:T(8,128)S(1)}, f32[8,8,128,128]{3,2,1,0:T(8,128)}, ...), condition=%wide.region_3.4_spmd.clone, body=%wide.region_2.3_spmd.clone.sunk | while | flops 524292 | bytes 1573073 | solution.py:18
  418.8 1.2 fusion.24
  420.0 1.2 fusion.24
  421.2 1.2 fusion.24
  422.5 1.2 fusion.24
  423.7 1.2 fusion.24
  424.9 1.2 fusion.24
  426.1 1.2 fusion.24
  427.3 0.0 copy-start.1
  427.3 4.0 multiply_reduce_fusion
  431.3 0.3 fusion.6
  431.6 1.3 copy.31
  (18 shorter events, 0.1 us)
Async XLA Ops:
  6.5 0.8 copy-start
  6.5 326.2 %all-gather.5.cloned.1.call-start = ((), (), s32[]{:S(2)}) async-start(), calls=%async_computation | async-start | bytes 42467328 | tf_op jit(solution)/shard_map/all_gather | solution.py:64
  7.3 411.5 %all-gather.7.cloned.1.call-start = ((), (), s32[]{:S(2)}) async-start(), calls=%async_computation.1 | async-start | bytes 4718592 | tf_op jit(solution)/shard_map/all_gather | solution.py:9
  366.9 4.8 %copy-start.2 = (u32[32]{0:T(128)S(1)}, u32[32]{0:T(128)}, u32[]{:S(2)}) copy-start(u32[32]{0:T(128)} %constant.44) | copy-start | bytes 388
  427.3 4.0 copy-start.1
Sparse Core Ops, SparseCore 0:
  9.0 323.7 all-gather.4
  371.8 46.9 all-gather.6
where the time goes:
time: 443 us; the launch traced here: 440 us
  waiting for transfers between devices  352 us (79%)
  matrix products  42.6 us (10%)
  between operations  14.1 us (3%)
  blocking collectives  12 us (3%)
  other arithmetic  9.99 us (2%)
  local copies, waits for them, and re-layouts  8.71 us (2%)
    all_gather x1, waiting for transfers between devices, shards(): lax.all_gather(qkv_weight, 'seq', axis=1, tiled=True)  324 us
    dot_general x1, matrix products, shards(): jnp.dot(inputs, lax.all_gather(qkv_weight, 'seq', axis=1, tiled=True), pr...  28.1 us
    all_gather x1, waiting for transfers between devices, prefix_2(): pieces = jax.tree.map(lambda part: lax.all_gather(part, axis), value)  27.7 us
    unnamed x1, blocking collectives  12 us
  transfers between devices with their start and end apart: 2, of which 2 were waited for; matrix products, arithmetic and copies ran while one was open for 2% of the time, Pallas kernels for 0%

commit v1 on v0

--- a/solution.py
+++ b/solution.py
@@ -1,7 +1,14 @@
+import functools
+
 import jax
 import jax.numpy as jnp
 from jax import lax
+from jax.experimental import pallas as pl
+from jax.experimental.pallas import tpu as pltpu
 from jax.sharding import PartitionSpec as P
+
+MESH = pl.DeviceIdType.MESH
+SUBS = 4
 
 
 def prefix_2(value, axis, join, neutral):
@@ -18,8 +25,13 @@
     return lax.fori_loop(0, count - 1, turn, subtotal)
 
 
-def block_terms(queries, keys, values, block_decay):
-    cumulated = jnp.cumsum(block_decay, axis=-1)
+def running(decays):
+    index = jnp.arange(decays.shape[-1])
+    upto = (index[:, None] <= index[None, :]).astype(jnp.float32)
+    return jnp.dot(decays, upto, precision=lax.Precision.HIGHEST)
+
+
+def block_terms(queries, keys, values, cumulated):
     tok_count = queries.shape[-2]
     row_index = jnp.arange(tok_count)[:, None]
     col_index = jnp.arange(tok_count)[None, :]
@@ -55,7 +67,7 @@
     )
 
 
-def shards(inputs, qkv_weight, log_decay, out_gain):
+def shards_wide(inputs, qkv_weight, log_decay, out_gain):
     tok_count = inputs.shape[0]
     local_heads = out_gain.shape[0]
     head_size = out_gain.shape[1]
@@ -67,7 +79,7 @@
     activated = jax.nn.silu(projected).astype(jnp.bfloat16)
     grouped = jnp.transpose(activated.reshape(tok_count, local_heads, 3, head_size), (2, 1, 0, 3))
     intra_term, update, block_total, queries_decayed = block_terms(
-        grouped[0], grouped[1], grouped[2], log_decay
+        grouped[0], grouped[1], grouped[2], running(log_decay)
     )
     identity = (jnp.zeros_like(block_total), jnp.zeros_like(update))
     prefix = prefix_2((block_total, update), "seq", chain_combine, identity)
@@ -79,7 +91,464 @@
     )
 
 
+def place():
+    dp, seq = lax.axis_index("dp"), lax.axis_index("seq")
+    return dp, seq, dp // 2, dp % 2, seq // 2, seq % 2
+
+
+def gather_kernel(
+    line, x_ref, w_ref, out, xg, wg, total,
+    own_send, own_recv, first_send, z_send, z_recv, y_send, y_recv,
+    wx_send, wx_recv, wf_send, wf_recv, wp_send, wp_recv, local_sem,
+):
+    dp, seq, y, x, z, c = place()
+    rows = x_ref.shape[0] // 2
+    half = rows // 2
+    sub = half // SUBS
+    width = w_ref.shape[1]
+    pieces = (line - 1) * SUBS
+    depth = w_ref.shape[0] // pieces
+    x_pair = {"dp": dp + 1 - 2 * x, "seq": seq}
+    y_pair = {"dp": dp + 2 - 4 * y, "seq": seq}
+    c_pair = {"dp": dp, "seq": seq + 1 - 2 * c}
+
+    def at(position, core):
+        return {"dp": dp, "seq": 2 * position + core}
+
+    barrier = pltpu.get_barrier_semaphore()
+    for target in (x_pair, y_pair, c_pair):
+        pl.semaphore_signal(barrier, inc=1, device_id=target, device_id_type=MESH)
+    for step in (1, -1):
+        @pl.when((z + step >= 0) & (z + step < line))
+        def _():
+            for core in (0, 1):
+                pl.semaphore_signal(barrier, inc=1, device_id=at(z + step, core), device_id_type=MESH)
+    count = 3 + 2 * ((z > 0).astype(jnp.int32) + (z < line - 1).astype(jnp.int32))
+    pl.semaphore_wait(barrier, count)
+
+    def remote(src, dst, send, recv, target):
+        return pltpu.make_async_remote_copy(
+            src_ref=src, dst_ref=dst, send_sem=send, recv_sem=recv,
+            device_id=target, device_id_type=MESH,
+        )
+
+    def strip(position, side, r):
+        return xg.at[position, pl.ds(pl.multiple_of(side * half + r * sub, sub), sub)]
+
+    def first(core, step, r):
+        start = pl.multiple_of(core * rows + y * half + r * sub, sub)
+        return remote(
+            x_ref.at[pl.ds(start, sub)], strip(z, y, r),
+            first_send.at[core, (step + 1) // 2, r], z_recv.at[z, r], at(z + step, core),
+        )
+
+    def columns(xx, cc):
+        return pl.ds(pl.multiple_of((xx * 2 + cc) * width, 128), width)
+
+    def weight_first(j):
+        part = pl.ds(j * depth, depth)
+        return remote(
+            w_ref.at[part], wg.at[part, columns(x, c)], wx_send.at[j], wx_recv.at[j], x_pair
+        )
+
+    def weight_next(j):
+        part = wg.at[pl.ds(j * depth, depth), columns(1 - x, c)]
+        return remote(part, part, wf_send.at[j], wf_recv.at[j], c_pair)
+
+    def own_rows(core):
+        return x_ref.at[pl.ds(pl.multiple_of(core * rows, rows), rows)]
+
+    own_local = pltpu.make_async_copy(own_rows(c), xg.at[z], local_sem.at[0])
+    own_peer = remote(own_rows(1 - c), xg.at[z], own_send, own_recv, c_pair)
+    w_local = pltpu.make_async_copy(w_ref, wg.at[:, columns(x, c)], local_sem.at[1])
+    w_peer = remote(w_ref, wg.at[:, columns(x, c)], wp_send, wp_recv, c_pair)
+
+    def exists(position):
+        return (position >= 0) & (position < line)
+
+    for r in range(SUBS):
+        for step in (1, -1):
+            @pl.when((c == x) & exists(z + step))
+            def _():
+                for core in (0, 1):
+                    first(core, step, r).start()
+    for j in range(pieces):
+        weight_first(j).start()
+
+    @pl.when(c == x)
+    def _():
+        own_local.start()
+        own_peer.start()
+    w_peer.start()
+    w_local.start()
+
+    def z_next(origin, step, r):
+        part = strip(origin, y, r)
+        return remote(part, part, z_send.at[origin, r], z_recv.at[origin, r], at(z - step, c))
+
+    def y_next(origin, side, r):
+        part = strip(origin, side, r)
+        return remote(part, part, y_send.at[origin, r], y_recv.at[origin, r], y_pair)
+
+    model = w_ref.shape[0]
+    early = (line - 2) * SUBS * depth
+    tile = 2 * out.shape[4]
+
+    def project(position, xx, low, high, begin=False, resume=False):
+        def turn(n, carry):
+            start = pl.multiple_of(n * tile, 128)
+            cols = pl.ds(pl.multiple_of(xx * 2 * width + n * tile, 128), tile)
+            term = jnp.dot(
+                xg[position, :, low:high], wg[low:high, cols], preferred_element_type=jnp.float32
+            )
+            if begin:
+                total[position, :, pl.ds(start, tile)] = term
+                return carry
+            if resume:
+                term = term + total[position, :, pl.ds(start, tile)]
+            term = (term * jax.nn.sigmoid(term)).astype(out.dtype)
+            for i in (0, 1):
+                j = 2 * n + i
+                out[j % 3, position, 2 * xx + j // 3] = term[:, i * tile // 2 : (i + 1) * tile // 2]
+            return carry
+
+        lax.fori_loop(0, 2 * width // tile, turn, 0)
+
+    def around(k, act):
+        for step in (1, -1):
+            @pl.when(exists(z + step * k))
+            def _():
+                act(z + step * k)
+
+    def y_wait(k):
+        def act(origin):
+            for r in range(SUBS):
+                y_next(origin, 1 - y, r).wait_recv()
+
+        around(k, act)
+
+    @pl.when(c == x)
+    def _():
+        own_local.wait()
+
+    @pl.when(c != x)
+    def _():
+        own_peer.wait_recv()
+
+    w_local.wait()
+    w_peer.wait()
+    project(z, x, 0, model)
+
+    for k in range(1, line):
+        for r in range(SUBS):
+            for step in (1, -1):
+                origin = z + step * k
+
+                @pl.when(exists(origin))
+                def _():
+                    z_next(origin, step, r).wait_recv()
+                    y_next(origin, y, r).start()
+
+                    @pl.when(exists(z - step))
+                    def _():
+                        z_next(origin, step, r).start()
+            j = (k - 1) * SUBS + r
+            weight_first(j).wait_recv()
+            weight_next(j).start()
+            if k >= 2 and r == 1:
+                y_wait(k - 1)
+                around(k - 1, lambda origin: project(origin, x, 0, model))
+                if k == line - 1:
+                    around(k - 1, lambda origin: project(origin, 1 - x, 0, early, begin=True))
+        if k == line - 2:
+            for j in range((line - 2) * SUBS):
+                weight_next(j).wait_recv()
+            project(z, 1 - x, 0, early, begin=True)
+            for before in range(1, k):
+                around(before, lambda origin: project(origin, 1 - x, 0, early, begin=True))
+
+    for j in range((line - 2) * SUBS, pieces):
+        weight_next(j).wait_recv()
+    project(z, 1 - x, early, model, resume=True)
+    for k in range(1, line - 1):
+        around(k, lambda origin: project(origin, 1 - x, early, model, resume=True))
+    y_wait(line - 1)
+    around(line - 1, lambda origin: project(origin, x, 0, model))
+    around(line - 1, lambda origin: project(origin, 1 - x, 0, model))
+
+    for k in range(1, line):
+        for r in range(SUBS):
+            for step in (1, -1):
+                origin = z + step * k
+
+                @pl.when(exists(origin))
+                def _():
+                    y_next(origin, y, r).wait_send()
+
+                    @pl.when(exists(z - step))
+                    def _():
+                        z_next(origin, step, r).wait_send()
+            j = (k - 1) * SUBS + r
+            weight_first(j).wait_send()
+            weight_next(j).wait_send()
+    for r in range(SUBS):
+        for step in (1, -1):
+            @pl.when((c == x) & exists(z + step))
+            def _():
+                for core in (0, 1):
+                    first(core, step, r).wait_send()
+
+    @pl.when(c == x)
+    def _():
+        own_peer.wait_send()
+
+
+def gather(line, inputs, weight, head_size):
+    tok, depth = inputs.shape
+    dma = pltpu.SemaphoreType.DMA
+    pieces = (line - 1) * SUBS
+    width = weight.shape[1]
+    any_space = pl.BlockSpec(memory_space=pl.ANY)
+    return pl.pallas_call(
+        functools.partial(gather_kernel, line),
+        out_shape=jax.ShapeDtypeStruct((3, line, 4, tok // 2, head_size), inputs.dtype),
+        in_specs=[any_space] * 2,
+        out_specs=pl.BlockSpec(memory_space=pltpu.VMEM),
+        scratch_shapes=[
+            pltpu.VMEM((line, tok // 2, depth), inputs.dtype),
+            pltpu.VMEM((depth, 4 * width), weight.dtype),
+            pltpu.VMEM((line, tok // 2, 2 * width), jnp.float32),
+            dma, dma, dma((2, 2, SUBS)), dma((line, SUBS)), dma((line, SUBS)),
+            dma((line, SUBS)), dma((line, SUBS)),
+            dma((pieces,)), dma((pieces,)), dma((pieces,)), dma((pieces,)),
+            dma, dma, dma((2,)),
+        ],
+        compiler_params=pltpu.CompilerParams(
+            collective_id=0, has_side_effects=True, vmem_limit_bytes=50 << 20
+        ),
+        name="gather",
+    )(inputs, weight)
+
+
+def share_kernel(l_ref, g_ref, ld, gd, l_send, l_recv, g_send, g_recv, local_sem):
+    dp, seq, y, x, z, c = place()
+    seqs = ld.shape[1]
+
+    def device(xx, ss):
+        return {"dp": 2 * y + xx, "seq": ss}
+
+    def others(act):
+        for xx in (0, 1):
+            for ss in range(seqs):
+                @pl.when((xx != x) | (ss != seq))
+                def _():
+                    act(xx, ss)
+
+    barrier = pltpu.get_barrier_semaphore()
+    others(
+        lambda xx, ss: pl.semaphore_signal(
+            barrier, inc=1, device_id=device(xx, ss), device_id_type=MESH
+        )
+    )
+    pl.semaphore_wait(barrier, 2 * seqs - 1)
+
+    def push(xx, ss):
+        return pltpu.make_async_remote_copy(
+            src_ref=l_ref, dst_ref=ld.at[x, seq],
+            send_sem=l_send.at[xx, ss], recv_sem=l_recv.at[x, seq],
+            device_id=device(xx, ss), device_id_type=MESH,
+        )
+
+    def pull(xx, ss):
+        return pltpu.make_async_remote_copy(
+            src_ref=l_ref, dst_ref=ld.at[xx, ss],
+            send_sem=l_send.at[xx, ss], recv_sem=l_recv.at[xx, ss],
+            device_id=device(xx, ss), device_id_type=MESH,
+        )
+
+    gain = pltpu.make_async_remote_copy(
+        src_ref=g_ref, dst_ref=gd.at[x], send_sem=g_send, recv_sem=g_recv,
+        device_id=device(1 - x, seq), device_id_type=MESH,
+    )
+    l_local = pltpu.make_async_copy(l_ref, ld.at[x, seq], local_sem.at[0])
+    g_local = pltpu.make_async_copy(g_ref, gd.at[x], local_sem.at[1])
+    others(lambda xx, ss: push(xx, ss).start())
+    gain.start()
+    l_local.start()
+    g_local.start()
+    others(lambda xx, ss: pull(xx, ss).wait_recv())
+    others(lambda xx, ss: push(xx, ss).wait_send())
+    gain.wait()
+    l_local.wait()
+    g_local.wait()
+
+
+def share(seqs, log_decay, out_gain):
+    dma = pltpu.SemaphoreType.DMA
+    vmem = pl.BlockSpec(memory_space=pltpu.VMEM)
+    return pl.pallas_call(
+        share_kernel,
+        out_shape=(
+            jax.ShapeDtypeStruct((2, seqs) + log_decay.shape, log_decay.dtype),
+            jax.ShapeDtypeStruct((2,) + out_gain.shape, out_gain.dtype),
+        ),
+        in_specs=[vmem] * 2,
+        out_specs=(vmem, vmem),
+        scratch_shapes=[dma((2, seqs)), dma((2, seqs)), dma, dma, dma((2,))],
+        compiler_params=pltpu.CompilerParams(
+            collective_id=2, has_side_effects=True, vmem_limit_bytes=4 << 20
+        ),
+        name="share",
+    )(log_decay, out_gain)
+
+
+def scatter_kernel(line, tiles, out, send_sem, recv_sem, local_sem):
+    dp, seq, y, x, z, c = place()
+    rows, cols = tiles.shape[2], tiles.shape[3]
+
+    def device(xx, zz, cc):
+        return {"dp": 2 * y + xx, "seq": 2 * zz + cc}
+
+    barrier = pltpu.get_barrier_semaphore()
+    for zz in range(line):
+        for cc in (0, 1):
+            @pl.when((zz != z) | (cc != c) | (c != x))
+            def _():
+                pl.semaphore_signal(
+                    barrier, inc=1, device_id=device(c, zz, cc), device_id_type=MESH
+                )
+    pl.semaphore_wait(barrier, 2 * line - (c == x).astype(jnp.int32))
+
+    def area(zz, cc):
+        return out.at[
+            pl.ds(pl.multiple_of(cc * rows, rows), rows),
+            pl.ds(pl.multiple_of(zz * cols, 128), cols),
+        ]
+
+    def push(zz, xx):
+        return pltpu.make_async_remote_copy(
+            src_ref=tiles.at[zz, xx], dst_ref=area(z, c),
+            send_sem=send_sem.at[zz, xx], recv_sem=recv_sem.at[z, c],
+            device_id=device(xx, zz, x), device_id_type=MESH,
+        )
+
+    def pull(zz, cc):
+        return pltpu.make_async_remote_copy(
+            src_ref=tiles.at[0, 0], dst_ref=area(zz, cc),
+            send_sem=send_sem.at[0, 0], recv_sem=recv_sem.at[zz, cc],
+            device_id=device(1 - x, z, c), device_id_type=MESH,
+        )
+
+    local = pltpu.make_async_copy(tiles.at[z, x], area(z, c), local_sem)
+    own = c == x
+    for zz in range(line):
+        for xx in (0, 1):
+            @pl.when((zz != z) | (xx != x) | jnp.logical_not(own))
+            def _():
+                push(zz, xx).start()
+
+    @pl.when(own)
+    def _():
+        local.start()
+    for zz in range(line):
+        for cc in (0, 1):
+            @pl.when((zz != z) | (cc != c) | jnp.logical_not(own))
+            def _():
+                pull(zz, cc).wait_recv()
+    for zz in range(line):
+        for xx in (0, 1):
+            @pl.when((zz != z) | (xx != x) | jnp.logical_not(own))
+            def _():
+                push(zz, xx).wait_send()
+
+    @pl.when(own)
+    def _():
+        local.wait()
+
+
+def scatter(line, tiles):
+    dma = pltpu.SemaphoreType.DMA
+    _, _, rows, cols = tiles.shape
+    any_space = pl.BlockSpec(memory_space=pl.ANY)
+    return pl.pallas_call(
+        functools.partial(scatter_kernel, line),
+        out_shape=jax.ShapeDtypeStruct((2 * rows, line * cols), tiles.dtype),
+        in_specs=[any_space],
+        out_specs=any_space,
+        scratch_shapes=[dma((line, 2)), dma((line, 2)), dma],
+        compiler_params=pltpu.CompilerParams(
+            collective_id=1, has_side_effects=True, vmem_limit_bytes=1 << 20
+        ),
+        name="scatter",
+    )(tiles)
+
+
+def shards_quarter(inputs, qkv_weight, log_decay, out_gain):
+    dps, seqs = lax.axis_size("dp"), lax.axis_size("seq")
+    dp, seq, y, x, z, c = place()
+    line = seqs // 2
+    tok = inputs.shape[0]
+    chunk = tok // 2
+    local_heads, head_size = out_gain.shape
+    heads = 4
+    decays, gains = share(seqs, log_decay, out_gain)
+    decays = lax.dynamic_slice_in_dim(decays, 2 * z, 2, axis=2)
+    decays = jnp.transpose(decays, (1, 0, 2, 3)).reshape(line, 2, 2, 2, 2, chunk)
+    decays = jnp.transpose(decays, (0, 1, 4, 2, 3, 5)).reshape(line, 2, 2, heads, chunk)
+    gains = lax.dynamic_slice_in_dim(gains, 2 * z, 2, axis=1).reshape(heads, head_size)
+    totals = jnp.sum(decays, axis=-1)
+    mine = lax.dynamic_index_in_dim(decays, x, 1, keepdims=False)
+    mine = lax.dynamic_index_in_dim(mine, c, 1, keepdims=False)
+
+    grouped = gather(line, inputs, qkv_weight, head_size)
+    grouped = grouped.reshape(3, line * heads, chunk, head_size)
+    cumulated = running(mine.reshape(line * heads, chunk))
+    intra_term, update, _, queries_decayed = block_terms(
+        grouped[0], grouped[1], grouped[2], cumulated
+    )
+    update = update.reshape(line, heads, head_size, head_size)
+    flat = [(d, s) for d in range(dps) for s in range(seqs)]
+    core_pairs = [(d * seqs + s, d * seqs + (s ^ 1)) for d, s in flat]
+    x_pairs = [(d * seqs + s, (d ^ 1) * seqs + s) for d, s in flat]
+    other = lax.ppermute(update, ("dp", "seq"), core_pairs)
+    lower = jnp.where(c == 0, update, other)
+    upper = jnp.where(c == 0, other, update)
+    my_totals = lax.dynamic_index_in_dim(totals, x, 1, keepdims=False)
+    joined = jnp.exp(my_totals[:, 1])[..., None, None] * lower + upper
+    part = lax.dynamic_slice_in_dim(joined, 2 * c, 2, axis=1)
+    part = lax.ppermute(part, ("dp", "seq"), x_pairs)
+    part_other = lax.ppermute(part, ("dp", "seq"), core_pairs)
+    across = jnp.concatenate(
+        [jnp.where(c == 0, part, part_other), jnp.where(c == 0, part_other, part)], axis=1
+    )
+    state = jnp.zeros_like(update[0])
+    block_totals = totals[:, :, 0] + totals[:, :, 1]
+    carried = []
+    for zz in range(line):
+        starts = []
+        for xx in (0, 1):
+            starts.append(state)
+            term = jnp.where(x == xx, joined[zz], across[zz])
+            state = jnp.exp(block_totals[zz, xx])[:, None, None] * state + term
+        start = jnp.where(x == 0, starts[0], starts[1])
+        later = jnp.exp(my_totals[zz, 0])[:, None, None] * start + lower[zz]
+        carried.append(jnp.where(c == 0, start, later))
+    carried = jnp.concatenate(carried, axis=0)
+    normed = finish_heads(intra_term, queries_decayed, carried, jnp.tile(gains, (line, 1)))
+    tiles = normed.astype(jnp.bfloat16).reshape(line, 2, 2, chunk, head_size)
+    tiles = jnp.transpose(tiles, (0, 1, 3, 2, 4)).reshape(line, 2, chunk, 2 * head_size)
+    return scatter(line, tiles)
+
+
 def solution(mesh):
     in_specs = (P("seq", None), P(None, ("dp", "seq")), P("dp", "seq"), P("dp", None))
     out_specs = P("seq", "dp")
+
+    def shards(inputs, qkv_weight, log_decay, out_gain):
+        local_heads, head_size = out_gain.shape
+        whole_heads = qkv_weight.shape[1] == 3 * head_size
+        fits = whole_heads and local_heads == mesh.shape["seq"] and mesh.shape["dp"] == 4
+        body = shards_quarter if fits else shards_wide
+        return body(inputs, qkv_weight, log_decay, out_gain)
+
     return jax.shard_map(shards, mesh=mesh, in_specs=in_specs, out_specs=out_specs, check_vma=False)

time: 443 us -> 212 us (0.48)
  waiting for transfers between devices: 352 us -> 14.8 us
  Pallas kernels: 0 us -> 172 us
  matrix products: 42.6 us -> 9.02 us
  between operations: 14.1 us -> 0.21 us
  blocking collectives: 12 us -> 0 us
  other arithmetic: 9.99 us -> 5.33 us
    all_gather x2 -> x0, waiting for transfers between devices: 351 us -> none  [the longest x1 324 us: shards(): lax.all_gather(qkv_weight, 'seq', axis=1, tiled=True)]
    pallas_call x0 -> x3, Pallas kernels: none -> 172 us  [the longest x1 134 us: gather(): pl.pallas_call(functools.partial(gather_kernel, line), out_shape=jax.Shap...]
    dot_general x1, matrix products: 28.1 us -> 0.15 us  [running(): return jnp.dot(decays, upto, precision=lax.Precision.HIGHEST)]
    ppermute x0 -> x3, waiting for transfers between devices: none -> 14.8 us  [the longest x1 12.4 us: shards_quarter(): part = lax.ppermute(part, ('dp', 'seq'), x_pairs)]
    unnamed x1 -> x0, blocking collectives: 12 us -> none
    select_n x7 -> x4, other arithmetic: 8.23 us -> 1.95 us  [the longest x1 1.37 us: shards_quarter(): jnp.where(c == 0, part, part_other)]
    convert_element_type x2 -> x0, local copies, waits for them, and re-layouts: 4.5 us -> none  [the longest x1 3.18 us: shards(): activated = jax.nn.silu(projected).astype(jnp.bfloat16)]
  transfers between devices with their start and end apart: 2 -> 3, of which waited for: 2 -> 2; matrix products, arithmetic and copies ran while one was open for 2% -> 2% of each run, Pallas kernels for 0% -> 0%
where the time goes in v1:
time: 212 us
  Pallas kernels  172 us (81%)
  waiting for transfers between devices  14.8 us (7%)
  matrix products  9.02 us (4%)
  local copies, waits for them, and re-layouts  8.4 us (4%)
  other arithmetic  5.33 us (3%)
  starting transfers between devices  2.14 us (1%)
    pallas_call x1, Pallas kernels, gather(): pl.pallas_call(functools.partial(gather_kernel, line), out_shape=jax.Shap...  134 us
    pallas_call x1, Pallas kernels, scatter(): pl.pallas_call(functools.partial(scatter_kernel, line), out_shape=jax.Sha...  26.4 us
    ppermute x1, waiting for transfers between devices, shards_quarter(): part = lax.ppermute(part, ('dp', 'seq'), x_pairs)  12.4 us
    pallas_call x1, Pallas kernels, share(): pl.pallas_call(share_kernel, out_shape=(jax.ShapeDtypeStruct((2, seqs) +...  11.1 us
    dot_general x1, matrix products, block_terms(): jnp.einsum('hts,hsd->htd', weights, values, preferred_element_type=jnp.fl...  4.41 us
  transfers between devices with their start and end apart: 3, of which 2 were waited for; matrix products, arithmetic and copies ran while one was open for 2% of the time, Pallas kernels for 0%

profile of v1, /device:TPU:11, one launch (start us, length us, event | category | flops | bytes accessed | tf_op | source)
XLA Modules:
  0.0 211.8 jit_solution(17881279547985199282)
XLA Ops:
  0.0 0.7 copy-done
  0.7 0.7 copy-done.1
  1.4 11.1 %share.1 = (f32[2,8,8,512]{3,2,1,0:T(8,128)S(1)}, f32[2,8,128]{2,1,0:T(8,128)S(1)}) custom-call(f32[8,512]{1,0:T(8,128)S(1)} %copy-done, f32[8,128]{1,0:T(8,128)S(1)} %copy-done.1), custom_call_target="tpu_custom_call" | custom-call | tf_op jit(solution)/shard_map/share/pallas_call | solution.py:389
  12.7 0.1 fusion.34
  12.8 0.2 slice_reduce_fusion
  13.1 134.5 %gather.1 = bf16[3,4,4,256,128]{4,3,2,1,0:T(8,128)(2,1)S(1)} custom-call(bf16[512,6144]{1,0:T(8,128)(2,1)} %x_ref.1, bf16[6144,384]{1,0:T(8,128)(2,1)} %w_ref.1), custom_call_target="tpu_custom_call" | custom-call | tf_op jit(solution)/shard_map/gather/pallas_call | solution.py:312
  147.6 1.2 fusion.49
  148.8 2.0 fusion
  150.9 0.1 bitcast_reduce_fusion
  151.0 0.1 copy.24
  151.2 0.1 copy.26
  151.3 2.4 %collective-permute-done = f32[4,4,128,128]{2,3,1,0:T(8,128)} collective-permute-done((f32[4,4,128,128]{2,3,1,0:T(8,128)S(1)}, f32[4,4,128,128]{2,3,1,0:T(8,128)}, u32[]{:S(2)}, u32[]{:S(2)}) %collective-permute-start) | collective-permute-done | bytes 1048608 | tf_op jit(solution)/shard_map/ppermute | solution.py:513
  153.7 2.8 %select_add_fusion = (f32[4,4,128,128]{2,3,1,0:T(8,128)S(1)}, f32[4,4,128,128]{2,3,1,0:T(8,128)}) fusion(f32[4,4,128,128]{2,3,1,0:T(8,128)} %collective-permute-done, f32[4,4,128,128]{2,3,1,0:T(8,128)} %bitcast.116, f32[4,4]{1,0:T(4,128)S(1)} %bitcast.127, pred[]{:T(512)S(6)} %eq.9), kind=kLoop, calls=%fused_computation.24 | loop fusion | flops 1048576 | bytes 4194369 | tf_op jit(solution)/shard_map/add | solution.py:517
  156.4 0.8 constant_dynamic-slice_fusion.1
  157.3 1.1 collective-permute-start.1
  158.4 0.1 copy.25
  158.5 12.4 %collective-permute-done.1 = f32[4,2,128,128]{2,3,1,0:T(8,128)} collective-permute-done((f32[4,2,128,128]{2,3,1,0:T(8,128)}, f32[4,2,128,128]{2,3,1,0:T(8,128)}, u32[]{:S(2)}, u32[]{:S(2)}) %collective-permute-start.1) | collective-permute-done | bytes 524320 | tf_op jit(solution)/shard_map/ppermute | solution.py:519
  171.0 1.0 collective-permute-start.2
  171.9 4.4 %fusion.9 = f32[16,256,128]{1,2,0:T(8,128)} fusion(bf16[16,256,128]{2,1,0:T(8,128)(2,1)S(1)} %bitcast.114, bf16[16,256,128]{2,1,0:T(8,128)(2,1)} %bitcast.118, bf16[16,256,128]{2,1,0:T(8,128)(2,1)S(1)} %bitcast.112, f32[16,256]{1,0:T(8,128)S(1)} %fusion.34, pred[256,256]{1,0:T(8,128)(4,1)S(1)} %iota_compare_fusion.1), kind=kOutput, calls=%fused_computation.10 | convolution fusion | flops 542113792 | bytes 5324800 | tf_op jit(solution)/shard_map/hts,hsd->htd/dot_general | solution.py:43
  176.3 1.4 broadcast_select_fusion.2
  177.7 0.2 copy-done.2
  177.9 0.2 fusion.31
  178.1 0.2 fusion.29
  178.3 0.2 fusion.23
  178.5 0.8 copy-done.4
  179.3 0.7 copy-done.5
  180.0 2.5 %multiply_reduce_fusion = (f32[16,256]{1,0:T(8,128)S(1)}, f32[16,256,128]{1,2,0:T(8,128)S(1)}) fusion(f32[16,256,128]{1,2,0:T(8,128)S(1)} %copy-done.5, f32[4,128,128]{1,2,0:T(8,128)S(1)} %fusion.23, f32[4,128,128]{1,2,0:T(8,128)S(1)} %get-tuple-element.11, f32[4,128,128]{1,2,0:T(8,128)S(1)} %get-tuple-element.9, f32[4,128,128]{1,2,0:T(8,128)S(1)} %get-tuple-element.13, ...), kind=kOutput, calls=%fused_computation.2 | convolution fusion | flops 808710144 | bytes 6324224 | tf_op jit(solution)/shard_map/htd,hde->hte/dot_general | solution.py:55
  182.6 0.3 multiply_convert_fusion.1
  182.9 0.8 copy.31
  183.7 0.7 reshape.141.tiles
  184.4 26.4 %scatter.1 = bf16[512,1024]{1,0:T(8,128)(2,1)S(1)} custom-call(bf16[4,2,256,256]{3,2,1,0:T(8,128)(2,1)S(1)} %reshape.141.tiles), custom_call_target="tpu_custom_call" | custom-call | tf_op jit(solution)/shard_map/scatter/pallas_call | solution.py:473
  210.8 1.0 copy.37
  (23 shorter events, 0.4 us)
Async XLA Ops:
  0.0 0.7 copy-start
  0.7 0.7 copy-start.1
  150.8 2.9 %copy-start.3 = (f32[16,128,128]{1,2,0:T(8,128)}, f32[16,128,128]{1,2,0:T(8,128)S(1)}, u32[]{:S(2)}) copy-start(f32[16,128,128]{1,2,0:T(8,128)S(1)} %fusion) | copy-start | bytes 3145732
  150.8 2.9 %collective-permute-start = (f32[4,4,128,128]{2,3,1,0:T(8,128)S(1)}, f32[4,4,128,128]{2,3,1,0:T(8,128)}, u32[]{:S(2)}, u32[]{:S(2)}) collective-permute-start(f32[4,4,128,128]{2,3,1,0:T(8,128)S(1)} %bitcast.115), channel_id=1, source_target_pairs={{0,1},{1,0},{2,3},{3,2},{4,5},{5,4},{6,7},{7,6},{8,9},{9,8},{10,11... | collective-permute-start | bytes 3145736 | tf_op jit(solution)/shard_map/ppermute | solution.py:513
  157.3 13.7 %collective-permute-start.1 = (f32[4,2,128,128]{2,3,1,0:T(8,128)}, f32[4,2,128,128]{2,3,1,0:T(8,128)}, u32[]{:S(2)}, u32[]{:S(2)}) collective-permute-start(f32[4,2,128,128]{2,3,1,0:T(8,128)} %constant_dynamic-slice_fusion.1), channel_id=1, source_target_pairs={{0,8},{1,9},{2,10},{3,11},{4,12},{5,13},{6,14},{7,15},{8,0},{9,1},... | collective-permute-start | bytes 1572872 | tf_op jit(solution)/shard_map/ppermute | solution.py:519
  171.0 5.4 %collective-permute-start.2 = (f32[4,2,128,128]{2,3,1,0:T(8,128)}, f32[4,2,128,128]{2,3,1,0:T(8,128)}, u32[]{:S(2)}, u32[]{:S(2)}) collective-permute-start(f32[4,2,128,128]{2,3,1,0:T(8,128)} %collective-permute-done.1), channel_id=1, source_target_pairs={{0,1},{1,0},{2,3},{3,2},{4,5},{5,4},{6,7},{7,6},{8,9},{9,8},{10,11... | collective-permute-start | bytes 1572872 | tf_op jit(solution)/shard_map/ppermute | solution.py:520
  176.3 1.5 copy-start.2
  178.1 1.2 copy-start.4
  178.1 1.9 copy-start.5

commit v2 on v1

--- a/solution.py
+++ b/solution.py
@@ -97,8 +97,8 @@
 
 
 def gather_kernel(
-    line, x_ref, w_ref, out, xg, wg, total,
-    own_send, own_recv, first_send, z_send, z_recv, y_send, y_recv,
+    line, x_ref, w_ref, l_ref, g_ref, out, ld, gd, xg, wg, total,
+    l_send, l_recv, g_send, g_recv, l_local_sem, own_send, own_recv, first_send, z_send, z_recv, y_send, y_recv,
     wx_send, wx_recv, wf_send, wf_recv, wp_send, wp_recv, local_sem,
 ):
     dp, seq, y, x, z, c = place()
@@ -115,17 +115,47 @@
     def at(position, core):
         return {"dp": dp, "seq": 2 * position + core}
 
+    seqs = ld.shape[1]
+
+    def device(xx, ss):
+        return {"dp": 2 * y + xx, "seq": ss}
+
+    def others(act):
+        for xx in (0, 1):
+            for ss in range(seqs):
+                @pl.when((xx != x) | (ss != seq))
+                def _():
+                    act(xx, ss)
+
     barrier = pltpu.get_barrier_semaphore()
-    for target in (x_pair, y_pair, c_pair):
-        pl.semaphore_signal(barrier, inc=1, device_id=target, device_id_type=MESH)
-    for step in (1, -1):
-        @pl.when((z + step >= 0) & (z + step < line))
-        def _():
-            for core in (0, 1):
-                pl.semaphore_signal(barrier, inc=1, device_id=at(z + step, core), device_id_type=MESH)
-    count = 3 + 2 * ((z > 0).astype(jnp.int32) + (z < line - 1).astype(jnp.int32))
-    pl.semaphore_wait(barrier, count)
-
+    others(
+        lambda xx, ss: pl.semaphore_signal(
+            barrier, inc=1, device_id=device(xx, ss), device_id_type=MESH
+        )
+    )
+    pl.semaphore_signal(barrier, inc=1, device_id=y_pair, device_id_type=MESH)
+    pl.semaphore_wait(barrier, 2 * seqs)
+
+    def push(xx, ss):
+        return pltpu.make_async_remote_copy(
+            src_ref=l_ref, dst_ref=ld.at[x, seq],
+            send_sem=l_send.at[xx, ss], recv_sem=l_recv.at[x, seq],
+            device_id=device(xx, ss), device_id_type=MESH,
+        )
+
+    def pull(xx, ss):
+        return pltpu.make_async_remote_copy(
+            src_ref=l_ref, dst_ref=ld.at[xx, ss],
+            send_sem=l_send.at[xx, ss], recv_sem=l_recv.at[xx, ss],
+            device_id=device(xx, ss), device_id_type=MESH,
+        )
+
+    gain = pltpu.make_async_remote_copy(
+        src_ref=g_ref, dst_ref=gd.at[x], send_sem=g_send, recv_sem=g_recv,
+        device_id=device(1 - x, seq), device_id_type=MESH,
+    )
+    l_local = pltpu.make_async_copy(l_ref, ld.at[x, seq], l_local_sem.at[0])
+    g_local = pltpu.make_async_copy(g_ref, gd.at[x], l_local_sem.at[1])
     def remote(src, dst, send, recv, target):
         return pltpu.make_async_remote_copy(
             src_ref=src, dst_ref=dst, send_sem=send, recv_sem=recv,
@@ -181,6 +211,10 @@
         own_peer.start()
     w_peer.start()
     w_local.start()
+    others(lambda xx, ss: push(xx, ss).start())
+    gain.start()
+    l_local.start()
+    g_local.start()
 
     def z_next(origin, step, r):
         part = strip(origin, y, r)
@@ -301,23 +335,35 @@
     @pl.when(c == x)
     def _():
         own_peer.wait_send()
-
-
-def gather(line, inputs, weight, head_size):
+    others(lambda xx, ss: pull(xx, ss).wait_recv())
+    others(lambda xx, ss: push(xx, ss).wait_send())
+    gain.wait()
+    l_local.wait()
+    g_local.wait()
+
+
+def gather(line, inputs, weight, log_decay, out_gain):
     tok, depth = inputs.shape
     dma = pltpu.SemaphoreType.DMA
     pieces = (line - 1) * SUBS
     width = weight.shape[1]
+    head_size = out_gain.shape[1]
     any_space = pl.BlockSpec(memory_space=pl.ANY)
+    vmem = pl.BlockSpec(memory_space=pltpu.VMEM)
     return pl.pallas_call(
         functools.partial(gather_kernel, line),
-        out_shape=jax.ShapeDtypeStruct((3, line, 4, tok // 2, head_size), inputs.dtype),
-        in_specs=[any_space] * 2,
-        out_specs=pl.BlockSpec(memory_space=pltpu.VMEM),
+        out_shape=(
+            jax.ShapeDtypeStruct((3, line, 4, tok // 2, head_size), inputs.dtype),
+            jax.ShapeDtypeStruct((2, 2 * line) + log_decay.shape, log_decay.dtype),
+            jax.ShapeDtypeStruct((2,) + out_gain.shape, out_gain.dtype),
+        ),
+        in_specs=[any_space, any_space, vmem, vmem],
+        out_specs=(vmem, vmem, vmem),
         scratch_shapes=[
             pltpu.VMEM((line, tok // 2, depth), inputs.dtype),
             pltpu.VMEM((depth, 4 * width), weight.dtype),
             pltpu.VMEM((line, tok // 2, 2 * width), jnp.float32),
+            dma((2, 2 * line)), dma((2, 2 * line)), dma, dma, dma((2,)),
             dma, dma, dma((2, 2, SUBS)), dma((line, SUBS)), dma((line, SUBS)),
             dma((line, SUBS)), dma((line, SUBS)),
             dma((pieces,)), dma((pieces,)), dma((pieces,)), dma((pieces,)),
@@ -327,79 +373,7 @@
             collective_id=0, has_side_effects=True, vmem_limit_bytes=50 << 20
         ),
         name="gather",
-    )(inputs, weight)
-
-
-def share_kernel(l_ref, g_ref, ld, gd, l_send, l_recv, g_send, g_recv, local_sem):
-    dp, seq, y, x, z, c = place()
-    seqs = ld.shape[1]
-
-    def device(xx, ss):
-        return {"dp": 2 * y + xx, "seq": ss}
-
-    def others(act):
-        for xx in (0, 1):
-            for ss in range(seqs):
-                @pl.when((xx != x) | (ss != seq))
-                def _():
-                    act(xx, ss)
-
-    barrier = pltpu.get_barrier_semaphore()
-    others(
-        lambda xx, ss: pl.semaphore_signal(
-            barrier, inc=1, device_id=device(xx, ss), device_id_type=MESH
-        )
-    )
-    pl.semaphore_wait(barrier, 2 * seqs - 1)
-
-    def push(xx, ss):
-        return pltpu.make_async_remote_copy(
-            src_ref=l_ref, dst_ref=ld.at[x, seq],
-            send_sem=l_send.at[xx, ss], recv_sem=l_recv.at[x, seq],
-            device_id=device(xx, ss), device_id_type=MESH,
-        )
-
-    def pull(xx, ss):
-        return pltpu.make_async_remote_copy(
-            src_ref=l_ref, dst_ref=ld.at[xx, ss],
-            send_sem=l_send.at[xx, ss], recv_sem=l_recv.at[xx, ss],
-            device_id=device(xx, ss), device_id_type=MESH,
-        )
-
-    gain = pltpu.make_async_remote_copy(
-        src_ref=g_ref, dst_ref=gd.at[x], send_sem=g_send, recv_sem=g_recv,
-        device_id=device(1 - x, seq), device_id_type=MESH,
-    )
-    l_local = pltpu.make_async_copy(l_ref, ld.at[x, seq], local_sem.at[0])
-    g_local = pltpu.make_async_copy(g_ref, gd.at[x], local_sem.at[1])
-    others(lambda xx, ss: push(xx, ss).start())
-    gain.start()
-    l_local.start()
-    g_local.start()
-    others(lambda xx, ss: pull(xx, ss).wait_recv())
-    others(lambda xx, ss: push(xx, ss).wait_send())
-    gain.wait()
-    l_local.wait()
-    g_local.wait()
-
-
-def share(seqs, log_decay, out_gain):
-    dma = pltpu.SemaphoreType.DMA
-    vmem = pl.BlockSpec(memory_space=pltpu.VMEM)
-    return pl.pallas_call(
-        share_kernel,
-        out_shape=(
-            jax.ShapeDtypeStruct((2, seqs) + log_decay.shape, log_decay.dtype),
-            jax.ShapeDtypeStruct((2,) + out_gain.shape, out_gain.dtype),
-        ),
-        in_specs=[vmem] * 2,
-        out_specs=(vmem, vmem),
-        scratch_shapes=[dma((2, seqs)), dma((2, seqs)), dma, dma, dma((2,))],
-        compiler_params=pltpu.CompilerParams(
-            collective_id=2, has_side_effects=True, vmem_limit_bytes=4 << 20
-        ),
-        name="share",
-    )(log_decay, out_gain)
+    )(inputs, weight, log_decay, out_gain)
 
 
 def scatter_kernel(line, tiles, out, send_sem, recv_sem, local_sem):
@@ -491,7 +465,7 @@
     chunk = tok // 2
     local_heads, head_size = out_gain.shape
     heads = 4
-    decays, gains = share(seqs, log_decay, out_gain)
+    grouped, decays, gains = gather(line, inputs, qkv_weight, log_decay, out_gain)
     decays = lax.dynamic_slice_in_dim(decays, 2 * z, 2, axis=2)
     decays = jnp.transpose(decays, (1, 0, 2, 3)).reshape(line, 2, 2, 2, 2, chunk)
     decays = jnp.transpose(decays, (0, 1, 4, 2, 3, 5)).reshape(line, 2, 2, heads, chunk)
@@ -500,7 +474,6 @@
     mine = lax.dynamic_index_in_dim(decays, x, 1, keepdims=False)
     mine = lax.dynamic_index_in_dim(mine, c, 1, keepdims=False)
 
-    grouped = gather(line, inputs, qkv_weight, head_size)
     grouped = grouped.reshape(3, line * heads, chunk, head_size)
     cumulated = running(mine.reshape(line * heads, chunk))
     intra_term, update, _, queries_decayed = block_terms(

time: 212 us -> 204 us (0.962)
  Pallas kernels: 172 us -> 163 us
    pallas_call x2 -> x1, Pallas kernels: 146 us -> 137 us  [gather(): pl.pallas_call(functools.partial(gather_kernel, line), out_shape=(jax.Sha...]
where the time goes in v2:
time: 204 us; the launch traced here: 203 us
  Pallas kernels  163 us (80%)
  waiting for transfers between devices  14.5 us (7%)
  matrix products  8.99 us (4%)
  local copies, waits for them, and re-layouts  8.42 us (4%)
  other arithmetic  5.33 us (3%)
  starting transfers between devices  2.45 us (1%)
    pallas_call x1, Pallas kernels, gather(): pl.pallas_call(functools.partial(gather_kernel, line), out_shape=(jax.Sha...  137 us
    pallas_call x1, Pallas kernels, scatter(): pl.pallas_call(functools.partial(scatter_kernel, line), out_shape=jax.Sha...  26.5 us
    ppermute x1, waiting for transfers between devices, shards_quarter(): part = lax.ppermute(part, ('dp', 'seq'), x_pairs)  12.1 us
    dot_general x1, matrix products, block_terms(): jnp.einsum('hts,hsd->htd', weights, values, preferred_element_type=jnp.fl...  4.36 us
  transfers between devices with their start and end apart: 3, of which 2 were waited for; matrix products, arithmetic and copies ran while one was open for 2% of the time, Pallas kernels for 0%

profile of v2, /device:TPU:11, one launch (start us, length us, event | category | flops | bytes accessed | tf_op | source)
XLA Modules:
  0.0 203.3 jit_solution(895213468671713990)
XLA Ops:
  0.0 0.7 copy-done
  0.7 0.7 copy-done.1
  1.4 136.9 %gather.1 = (bf16[3,4,4,256,128]{4,3,2,1,0:T(8,128)(2,1)S(1)}, f32[2,8,8,512]{3,2,1,0:T(8,128)S(1)}, f32[2,8,128]{2,1,0:T(8,128)S(1)}) custom-call(bf16[512,6144]{1,0:T(8,128)(2,1)} %x_ref.1, bf16[6144,384]{1,0:T(8,128)(2,1)} %w_ref.1, f32[8,512]{1,0:T(8,128)S(1)} %copy-done, f32[8,128]{1,0:T(8,128)S(1)} %copy-done.1), custom_call_target="tpu_custom_call" | custom-call | tf_op jit(solution)/shard_map/gather/pallas_call | solution.py:353
  138.3 1.2 fusion.49
  139.6 0.1 reshape.136
  139.8 0.1 fusion.34
  139.9 0.2 slice_reduce_fusion
  140.2 2.0 fusion
  142.3 0.1 bitcast_reduce_fusion
  142.4 0.1 copy.24
  142.6 0.1 copy.26
  142.7 2.4 %collective-permute-done = f32[4,4,128,128]{2,3,1,0:T(8,128)} collective-permute-done((f32[4,4,128,128]{2,3,1,0:T(8,128)S(1)}, f32[4,4,128,128]{2,3,1,0:T(8,128)}, u32[]{:S(2)}, u32[]{:S(2)}) %collective-permute-start) | collective-permute-done | bytes 1048608 | tf_op jit(solution)/shard_map/ppermute | solution.py:486
  145.1 2.8 %select_add_fusion = (f32[4,4,128,128]{2,3,1,0:T(8,128)S(1)}, f32[4,4,128,128]{2,3,1,0:T(8,128)}) fusion(f32[4,4,128,128]{2,3,1,0:T(8,128)} %collective-permute-done, f32[4,4,128,128]{2,3,1,0:T(8,128)} %bitcast.116, f32[4,4]{1,0:T(4,128)S(1)} %bitcast.127, pred[]{:T(512)S(6)} %eq.9), kind=kLoop, calls=%fused_computation.24 | loop fusion | flops 1048576 | bytes 4194369 | tf_op jit(solution)/shard_map/add | solution.py:490
  147.8 0.8 constant_dynamic-slice_fusion.1
  148.7 1.4 collective-permute-start.1
  150.1 0.1 copy.25
  150.3 12.1 %collective-permute-done.1 = f32[4,2,128,128]{2,3,1,0:T(8,128)} collective-permute-done((f32[4,2,128,128]{2,3,1,0:T(8,128)}, f32[4,2,128,128]{2,3,1,0:T(8,128)}, u32[]{:S(2)}, u32[]{:S(2)}) %collective-permute-start.1) | collective-permute-done | bytes 524320 | tf_op jit(solution)/shard_map/ppermute | solution.py:492
  162.4 1.0 collective-permute-start.2
  163.3 4.4 %fusion.9 = f32[16,256,128]{1,2,0:T(8,128)} fusion(bf16[16,256,128]{2,1,0:T(8,128)(2,1)S(1)} %bitcast.114, bf16[16,256,128]{2,1,0:T(8,128)(2,1)} %bitcast.118, bf16[16,256,128]{2,1,0:T(8,128)(2,1)S(1)} %bitcast.112, f32[16,256]{1,0:T(8,128)S(1)} %fusion.34, pred[256,256]{1,0:T(8,128)(4,1)S(1)} %iota_compare_fusion.1), kind=kOutput, calls=%fused_computation.10 | convolution fusion | flops 542113792 | bytes 5324800 | tf_op jit(solution)/shard_map/hts,hsd->htd/dot_general | solution.py:43
  167.7 1.4 broadcast_select_fusion.2
  169.1 0.2 copy-done.2
  169.2 0.2 fusion.31
  169.5 0.2 fusion.29
  169.7 0.2 fusion.23
  169.9 0.8 copy-done.4
  170.7 0.7 copy-done.5
  171.4 2.5 %multiply_reduce_fusion = (f32[16,256]{1,0:T(8,128)S(1)}, f32[16,256,128]{1,2,0:T(8,128)S(1)}) fusion(f32[16,256,128]{1,2,0:T(8,128)S(1)} %copy-done.5, f32[4,128,128]{1,2,0:T(8,128)S(1)} %fusion.23, f32[4,128,128]{1,2,0:T(8,128)S(1)} %get-tuple-element.13, f32[4,128,128]{1,2,0:T(8,128)S(1)} %get-tuple-element.11, f32[4,128,128]{1,2,0:T(8,128)S(1)} %get-tuple-element.15, ...), kind=kOutput, calls=%fused_computation.2 | convolution fusion | flops 808710144 | bytes 6324224 | tf_op jit(solution)/shard_map/htd,hde->hte/dot_general | solution.py:55
  173.9 0.3 multiply_convert_fusion.1
  174.3 0.8 copy.31
  175.1 0.7 reshape.141.tiles
  175.8 26.5 %scatter.1 = bf16[512,1024]{1,0:T(8,128)(2,1)S(1)} custom-call(bf16[4,2,256,256]{3,2,1,0:T(8,128)(2,1)S(1)} %reshape.141.tiles), custom_call_target="tpu_custom_call" | custom-call | tf_op jit(solution)/shard_map/scatter/pallas_call | solution.py:447
  202.4 1.0 copy.37
  (22 shorter events, 0.4 us)
Async XLA Ops:
  0.0 0.7 copy-start
  0.7 0.7 copy-start.1
  142.2 2.9 %copy-start.3 = (f32[16,128,128]{1,2,0:T(8,128)}, f32[16,128,128]{1,2,0:T(8,128)S(1)}, u32[]{:S(2)}) copy-start(f32[16,128,128]{1,2,0:T(8,128)S(1)} %fusion) | copy-start | bytes 3145732
  142.2 2.9 %collective-permute-start = (f32[4,4,128,128]{2,3,1,0:T(8,128)S(1)}, f32[4,4,128,128]{2,3,1,0:T(8,128)}, u32[]{:S(2)}, u32[]{:S(2)}) collective-permute-start(f32[4,4,128,128]{2,3,1,0:T(8,128)S(1)} %bitcast.115), channel_id=1, source_target_pairs={{0,1},{1,0},{2,3},{3,2},{4,5},{5,4},{6,7},{7,6},{8,9},{9,8},{10,11... | collective-permute-start | bytes 3145736 | tf_op jit(solution)/shard_map/ppermute | solution.py:486
  148.7 13.7 %collective-permute-start.1 = (f32[4,2,128,128]{2,3,1,0:T(8,128)}, f32[4,2,128,128]{2,3,1,0:T(8,128)}, u32[]{:S(2)}, u32[]{:S(2)}) collective-permute-start(f32[4,2,128,128]{2,3,1,0:T(8,128)} %constant_dynamic-slice_fusion.1), channel_id=1, source_target_pairs={{0,8},{1,9},{2,10},{3,11},{4,12},{5,13},{6,14},{7,15},{8,0},{9,1},... | collective-permute-start | bytes 1572872 | tf_op jit(solution)/shard_map/ppermute | solution.py:492
  162.4 5.3 %collective-permute-start.2 = (f32[4,2,128,128]{2,3,1,0:T(8,128)}, f32[4,2,128,128]{2,3,1,0:T(8,128)}, u32[]{:S(2)}, u32[]{:S(2)}) collective-permute-start(f32[4,2,128,128]{2,3,1,0:T(8,128)} %collective-permute-done.1), channel_id=1, source_target_pairs={{0,1},{1,0},{2,3},{3,2},{4,5},{5,4},{6,7},{7,6},{8,9},{9,8},{10,11... | collective-permute-start | bytes 1572872 | tf_op jit(solution)/shard_map/ppermute | solution.py:493
  167.7 1.5 copy-start.2
  169.5 1.2 copy-start.4
  169.5 1.9 copy-start.5

commit v3 on v2

--- a/solution.py
+++ b/solution.py
@@ -8,7 +8,7 @@
 from jax.sharding import PartitionSpec as P
 
 MESH = pl.DeviceIdType.MESH
-SUBS = 4
+SUBS = 8
 
 
 def prefix_2(value, axis, join, neutral):
@@ -289,7 +289,7 @@
             j = (k - 1) * SUBS + r
             weight_first(j).wait_recv()
             weight_next(j).start()
-            if k >= 2 and r == 1:
+            if k >= 2 and r == SUBS // 2 - 1:
                 y_wait(k - 1)
                 around(k - 1, lambda origin: project(origin, x, 0, model))
                 if k == line - 1:

time: 204 us -> 205 us (level)
  no operation moved by 1% of the time
where the time goes in v3:
time: 205 us
  Pallas kernels  165 us (80%)
  waiting for transfers between devices  14.5 us (7%)
  matrix products  8.99 us (4%)
  local copies, waits for them, and re-layouts  8.42 us (4%)
  other arithmetic  5.33 us (3%)
  starting transfers between devices  2.41 us (1%)
    pallas_call x1, Pallas kernels, gather(): pl.pallas_call(functools.partial(gather_kernel, line), out_shape=(jax.Sha...  138 us
    pallas_call x1, Pallas kernels, scatter(): pl.pallas_call(functools.partial(scatter_kernel, line), out_shape=jax.Sha...  26.5 us
    ppermute x1, waiting for transfers between devices, shards_quarter(): part = lax.ppermute(part, ('dp', 'seq'), x_pairs)  12.2 us
    dot_general x1, matrix products, block_terms(): jnp.einsum('hts,hsd->htd', weights, values, preferred_element_type=jnp.fl...  4.37 us
  transfers between devices with their start and end apart: 3, of which 2 were waited for; matrix products, arithmetic and copies ran while one was open for 2% of the time, Pallas kernels for 0%

profile of v3, /device:TPU:11, one launch (start us, length us, event | category | flops | bytes accessed | tf_op | source)
XLA Modules:
  0.0 204.8 jit_solution(4587874261538735777)
XLA Ops:
  0.0 0.7 copy-done
  0.7 0.7 copy-done.1
  1.4 138.4 %gather.1 = (bf16[3,4,4,256,128]{4,3,2,1,0:T(8,128)(2,1)S(1)}, f32[2,8,8,512]{3,2,1,0:T(8,128)S(1)}, f32[2,8,128]{2,1,0:T(8,128)S(1)}) custom-call(bf16[512,6144]{1,0:T(8,128)(2,1)} %x_ref.1, bf16[6144,384]{1,0:T(8,128)(2,1)} %w_ref.1, f32[8,512]{1,0:T(8,128)S(1)} %copy-done, f32[8,128]{1,0:T(8,128)S(1)} %copy-done.1), custom_call_target="tpu_custom_call" | custom-call | tf_op jit(solution)/shard_map/gather/pallas_call | solution.py:353
  139.8 1.2 fusion.49
  141.1 0.1 reshape.136
  141.2 0.1 fusion.34
  141.4 0.2 slice_reduce_fusion
  141.7 2.0 fusion
  143.8 0.1 bitcast_reduce_fusion
  143.9 0.1 copy.24
  144.0 0.1 copy.26
  144.2 2.4 %collective-permute-done = f32[4,4,128,128]{2,3,1,0:T(8,128)} collective-permute-done((f32[4,4,128,128]{2,3,1,0:T(8,128)S(1)}, f32[4,4,128,128]{2,3,1,0:T(8,128)}, u32[]{:S(2)}, u32[]{:S(2)}) %collective-permute-start) | collective-permute-done | bytes 1048608 | tf_op jit(solution)/shard_map/ppermute | solution.py:486
  146.5 2.8 %select_add_fusion = (f32[4,4,128,128]{2,3,1,0:T(8,128)S(1)}, f32[4,4,128,128]{2,3,1,0:T(8,128)}) fusion(f32[4,4,128,128]{2,3,1,0:T(8,128)} %collective-permute-done, f32[4,4,128,128]{2,3,1,0:T(8,128)} %bitcast.116, f32[4,4]{1,0:T(4,128)S(1)} %bitcast.127, pred[]{:T(512)S(6)} %eq.9), kind=kLoop, calls=%fused_computation.24 | loop fusion | flops 1048576 | bytes 4194369 | tf_op jit(solution)/shard_map/add | solution.py:490
  149.3 0.8 constant_dynamic-slice_fusion.1
  150.1 1.4 collective-permute-start.1
  151.5 0.1 copy.25
  151.7 12.2 %collective-permute-done.1 = f32[4,2,128,128]{2,3,1,0:T(8,128)} collective-permute-done((f32[4,2,128,128]{2,3,1,0:T(8,128)}, f32[4,2,128,128]{2,3,1,0:T(8,128)}, u32[]{:S(2)}, u32[]{:S(2)}) %collective-permute-start.1) | collective-permute-done | bytes 524320 | tf_op jit(solution)/shard_map/ppermute | solution.py:492
  163.8 1.0 collective-permute-start.2
  164.8 4.4 %fusion.9 = f32[16,256,128]{1,2,0:T(8,128)} fusion(bf16[16,256,128]{2,1,0:T(8,128)(2,1)S(1)} %bitcast.114, bf16[16,256,128]{2,1,0:T(8,128)(2,1)} %bitcast.118, bf16[16,256,128]{2,1,0:T(8,128)(2,1)S(1)} %bitcast.112, f32[16,256]{1,0:T(8,128)S(1)} %fusion.34, pred[256,256]{1,0:T(8,128)(4,1)S(1)} %iota_compare_fusion.1), kind=kOutput, calls=%fused_computation.10 | convolution fusion | flops 542113792 | bytes 5324800 | tf_op jit(solution)/shard_map/hts,hsd->htd/dot_general | solution.py:43
  169.2 1.4 broadcast_select_fusion.2
  170.6 0.2 copy-done.2
  170.7 0.2 fusion.31
  171.0 0.2 fusion.29
  171.1 0.2 fusion.23
  171.3 0.8 copy-done.4
  172.2 0.7 copy-done.5
  172.9 2.5 %multiply_reduce_fusion = (f32[16,256]{1,0:T(8,128)S(1)}, f32[16,256,128]{1,2,0:T(8,128)S(1)}) fusion(f32[16,256,128]{1,2,0:T(8,128)S(1)} %copy-done.5, f32[4,128,128]{1,2,0:T(8,128)S(1)} %fusion.23, f32[4,128,128]{1,2,0:T(8,128)S(1)} %get-tuple-element.13, f32[4,128,128]{1,2,0:T(8,128)S(1)} %get-tuple-element.11, f32[4,128,128]{1,2,0:T(8,128)S(1)} %get-tuple-element.15, ...), kind=kOutput, calls=%fused_computation.2 | convolution fusion | flops 808710144 | bytes 6324224 | tf_op jit(solution)/shard_map/htd,hde->hte/dot_general | solution.py:55
  175.4 0.3 multiply_convert_fusion.1
  175.7 0.8 copy.31
  176.6 0.7 reshape.141.tiles
  177.3 26.5 %scatter.1 = bf16[512,1024]{1,0:T(8,128)(2,1)S(1)} custom-call(bf16[4,2,256,256]{3,2,1,0:T(8,128)(2,1)S(1)} %reshape.141.tiles), custom_call_target="tpu_custom_call" | custom-call | tf_op jit(solution)/shard_map/scatter/pallas_call | solution.py:447
  203.8 1.0 copy.37
  (22 shorter events, 0.4 us)
Async XLA Ops:
  0.0 0.7 copy-start
  0.7 0.7 copy-start.1
  143.7 2.9 %copy-start.3 = (f32[16,128,128]{1,2,0:T(8,128)}, f32[16,128,128]{1,2,0:T(8,128)S(1)}, u32[]{:S(2)}) copy-start(f32[16,128,128]{1,2,0:T(8,128)S(1)} %fusion) | copy-start | bytes 3145732
  143.7 2.9 %collective-permute-start = (f32[4,4,128,128]{2,3,1,0:T(8,128)S(1)}, f32[4,4,128,128]{2,3,1,0:T(8,128)}, u32[]{:S(2)}, u32[]{:S(2)}) collective-permute-start(f32[4,4,128,128]{2,3,1,0:T(8,128)S(1)} %bitcast.115), channel_id=1, source_target_pairs={{0,1},{1,0},{2,3},{3,2},{4,5},{5,4},{6,7},{7,6},{8,9},{9,8},{10,11... | collective-permute-start | bytes 3145736 | tf_op jit(solution)/shard_map/ppermute | solution.py:486
  150.1 13.7 %collective-permute-start.1 = (f32[4,2,128,128]{2,3,1,0:T(8,128)}, f32[4,2,128,128]{2,3,1,0:T(8,128)}, u32[]{:S(2)}, u32[]{:S(2)}) collective-permute-start(f32[4,2,128,128]{2,3,1,0:T(8,128)} %constant_dynamic-slice_fusion.1), channel_id=1, source_target_pairs={{0,8},{1,9},{2,10},{3,11},{4,12},{5,13},{6,14},{7,15},{8,0},{9,1},... | collective-permute-start | bytes 1572872 | tf_op jit(solution)/shard_map/ppermute | solution.py:492
  163.8 5.3 %collective-permute-start.2 = (f32[4,2,128,128]{2,3,1,0:T(8,128)}, f32[4,2,128,128]{2,3,1,0:T(8,128)}, u32[]{:S(2)}, u32[]{:S(2)}) collective-permute-start(f32[4,2,128,128]{2,3,1,0:T(8,128)} %collective-permute-done.1), channel_id=1, source_target_pairs={{0,1},{1,0},{2,3},{3,2},{4,5},{5,4},{6,7},{7,6},{8,9},{9,8},{10,11... | collective-permute-start | bytes 1572872 | tf_op jit(solution)/shard_map/ppermute | solution.py:493
  169.2 1.5 copy-start.2
  170.9 1.2 copy-start.4
  170.9 1.9 copy-start.5
